TPU v7x, 512 devices: a whole 4x8x8 slice. The times are simulated.
512 devices in a mesh: group: 8 (over z_lo, x), fsdp: 64 (over y, z_hi, core).
Axes of the slice: x: 4, y: 8, z: 8 (z_hi: 4, z_lo: 2; z = z_hi * 2 + z_lo), core: 2. Of those that a mesh axis runs over, the one named last changes fastest.
Arguments:
- hidden: bfloat16 [8, 11776, 8192], P('group', 'fsdp'), may hold values from -6 to 6
- cotangent: bfloat16 [8, 11776, 512], P('group', 'fsdp'), may hold values from -0.4375 to 0.4375
- weight: float32 [8, 8192, 512], P('group', 'fsdp'), may hold values from -6 to 6
- first_moment: bfloat16 [8, 8192, 512], P('group', 'fsdp'), may hold values from -12 to 12
- second_moment: bfloat16 [8, 8192, 512], P('group', 'fsdp'), may hold values from 1 to 100
- sync_frag: int32 [1], replicated, may hold values from 0 to 5
- frag_local: float32 [8, 8192, 512], P('group', 'fsdp'), may hold values from -6 to 6
- frag_anchor: float32 [6, 8192, 512], P(None, ('fsdp', 'group')), may hold values from -6 to 6
- frag_momentum: float32 [6, 8192, 512], P(None, ('fsdp', 'group')), may hold values from -3 to 3
Outputs:
- new_weight: float32 [8, 8192, 512], P('group', 'fsdp')
- new_first: bfloat16 [8, 8192, 512], P('group', 'fsdp')
- new_second: bfloat16 [8, 8192, 512], P('group', 'fsdp')
- new_local: float32 [8, 8192, 512], P('group', 'fsdp')
- new_anchor: float32 [8192, 512], P(('fsdp', 'group'))
- new_momentum: float32 [8192, 512], P(('fsdp', 'group'))
All inputs are finite; a program needn't handle non-finite values.
Results may differ from a plain program's by a relative error of at most 0.0065.
Values may be sent and summed in bfloat16 or wider, within the bound.
A program may use at most 64 MiB of HBM per device.

v0:
```python
import jax
import jax.numpy as jnp
from jax import lax
from jax.sharding import PartitionSpec as P

beta_one = 0.9
beta_two = 0.95
bias_one = 1.0 - 0.9**10
bias_two = 1.0 - 0.95**10
inner_rate = 0.01
weight_decay = 0.1
epsilon = 1e-08
outer_rate = 0.7
outer_mu = 0.9
mixing = 0.5


def contract_tokens(features, cotans):
    return lax.dot_general(
        features, cotans, (((0,), (0,)), ((), ())), preferred_element_type=jnp.float32
    )


def per_device(
    hidden,
    cotangent,
    weight,
    first_moment,
    second_moment,
    sync_frag,
    frag_local,
    frag_anchor,
    frag_momentum,
):
    fsdp_count = lax.axis_size("fsdp")
    tokens = hidden[0]
    cotans = cotangent[0]
    count, width = tokens.shape
    stripe = width // fsdp_count
    outgoing = tokens.reshape(count, fsdp_count, stripe)
    columns = lax.all_to_all(outgoing, "fsdp", split_axis=1, concat_axis=0, tiled=True)[:, 0, :]
    gradient = contract_tokens(columns, lax.all_gather(cotans, "fsdp", axis=0, tiled=True))
    moment_one = beta_one * first_moment[0].astype(jnp.float32) + (1.0 - beta_one) * gradient
    moment_two = (
        beta_two * second_moment[0].astype(jnp.float32) + (1.0 - beta_two) * gradient * gradient
    )
    step_size = moment_one / bias_one / (jnp.sqrt(moment_two / bias_two) + epsilon)
    master = weight[0]
    new_weight = master - inner_rate * (step_size + weight_decay * master)
    group_count = lax.axis_size("group")
    chosen = sync_frag[0]
    local = frag_local[0]
    anchor = lax.dynamic_index_in_dim(frag_anchor, chosen, 0, keepdims=False)
    momentum = lax.dynamic_index_in_dim(frag_momentum, chosen, 0, keepdims=False)
    sublength = anchor.shape[0]
    anchor_full, momentum_full = (
        lax.all_gather(anchor.astype(jnp.bfloat16), "group", axis=0, tiled=True).astype(
            anchor.dtype
        ),
        lax.all_gather(momentum.astype(jnp.bfloat16), "group", axis=0, tiled=True).astype(
            momentum.dtype
        ),
    )
    local_sum = lax.psum(local, "group")
    mean_delta = anchor_full - local_sum / group_count
    momentum_next = outer_mu * momentum_full + mean_delta
    anchor_next = anchor_full - outer_rate * (mean_delta + outer_mu * momentum_next)
    offset = lax.axis_index("group") * sublength
    anchor_out = lax.dynamic_slice_in_dim(anchor_next, offset, sublength, 0)
    momentum_out = lax.dynamic_slice_in_dim(momentum_next, offset, sublength, 0)
    new_local = mixing * local + (1.0 - mixing) * anchor_next
    return (
        new_weight[None],
        moment_one.astype(jnp.bfloat16)[None],
        moment_two.astype(jnp.bfloat16)[None],
        new_local[None],
        anchor_out,
        momentum_out,
    )


def solution(mesh):
    in_specs = (
        P("group", "fsdp", None),
        P("group", "fsdp", None),
        P("group", "fsdp", None),
        P("group", "fsdp", None),
        P("group", "fsdp", None),
        P(),
        P("group", "fsdp", None),
        P(None, ("fsdp", "group"), None),
        P(None, ("fsdp", "group"), None),
    )
    out_specs = (
        P("group", "fsdp", None),
        P("group", "fsdp", None),
        P("group", "fsdp", None),
        P("group", "fsdp", None),
        P(("fsdp", "group"), None),
        P(("fsdp", "group"), None),
    )
    return jax.shard_map(
        per_device, mesh=mesh, in_specs=in_specs, out_specs=out_specs, check_vma=False
    )
```

profile of v0, /device:TPU:1, one launch (start us, length us, event | category | flops | bytes accessed | tf_op | source)
XLA Modules:
  0.0 223.5 jit_solution(8440201926474319656)
XLA Ops:
  8.0 0.0 copy-start
  8.0 0.0 all-reduce.2.cloned.1.call-start
  8.1 0.7 all-reduce.2.cloned.1.call-update
  8.7 0.0 all-gather.5.cloned.1.call-start
  8.8 0.5 all-gather.5.cloned.1.call-update
  9.3 2.7 %copy.17 = bf16[23,8,64,128]{3,2,1,0:T(8,128)(2,1)S(1)} copy(bf16[23,8,64,128]{3,1,2,0:T(8,128)(2,1)} %bitcast.69) | data formatting | bytes 6029312
  12.0 3.6 %copy.16 = bf16[184,64,128]{2,0,1:T(8,128)(2,1)} copy(bf16[184,64,128]{2,1,0:T(8,128)(2,1)S(1)} %bitcast.68) | data formatting | bytes 6029312 | tf_op jit(solution)/shard_map/reshape;squeeze | solution.py:40
  15.6 0.0 copy-start.1
  15.6 17.8 %all-to-all-start = ((bf16[184,64,128]{2,0,1:T(8,128)(2,1)}), bf16[184,64,128]{2,0,1:T(8,128)(2,1)S(1)}, u32[]{:S(2)}, u32[]{:S(2)}) async-start(bf16[184,64,128]{2,0,1:T(8,128)(2,1)} %copy.16), calls=%async_computation | async-start | bytes 6029312 | tf_op jit(solution)/shard_map/all_to_all | solution.py:41
  34.0 0.0 copy-done
  34.1 95.0 %all-gather.2 = bf16[1,128,512]{2,1,0:T(8,128)(2,1)} all-gather(bf16[1,16,512]{2,1,0:T(8,128)(2,1)S(1)} %dynamic-slice_convert_fusion), channel_id=4, replica_groups=mesh['group'=8,'fsdp'=64] {'group'}, dimensions={1}, use_global_device_ids=true | all-gather | bytes 147456 | tf_op jit(solution)/shard_map/all_gather | solution.py:60
  129.1 0.8 dynamic-slice_convert_fusion.1
  129.8 25.9 %all-gather.1 = bf16[1,128,512]{2,1,0:T(8,128)(2,1)} all-gather(bf16[1,16,512]{2,1,0:T(8,128)(2,1)S(1)} %dynamic-slice_convert_fusion.1), channel_id=3, replica_groups=mesh['group'=8,'fsdp'=64] {'group'}, dimensions={1}, use_global_device_ids=true | all-gather | bytes 147456 | tf_op jit(solution)/shard_map/all_gather | solution.py:57
  155.7 42.3 %all-reduce.2.cloned.1.call-done = f32[128,512]{1,0:T(8,128)} async-done(((f32[128,512]{1,0:T(8,128)}), f32[128,512]{1,0:T(8,128)}) %all-reduce.2.cloned.1.call-update) | async-done | bytes 262160 | tf_op jit(solution)/shard_map/psum | solution.py:64
  198.0 0.0 copy-done.1
  198.0 1.9 multiply_bitcast_fusion
  199.9 0.6 constant_dynamic-slice_fusion
  200.5 0.0 all-to-all-done
  200.5 8.3 %all-gather.5.cloned.1.call-done = bf16[1,11776,512]{2,1,0:T(8,128)(2,1)} async-done(((bf16[1,184,512]{2,1,0:T(8,128)(2,1)}), bf16[1,11776,512]{2,1,0:T(8,128)(2,1)}) %all-gather.5.cloned.1.call-update) | async-done | bytes 12058640 | tf_op jit(solution)/shard_map/all_gather | solution.py:42
  208.8 7.2 %fusion.8 = (bf16[1,128,512]{2,1,0:T(8,128)(2,1)}, f32[1,128,512]{2,1,0:T(8,128)}, bf16[1,128,512]{2,1,0:T(8,128)(2,1)}) fusion(bf16[1,128,512]{2,1,0:T(8,128)(2,1)} %param.13, bf16[1,128,512]{2,1,0:T(8,128)(2,1)} %param.12, f32[1,128,512]{2,1,0:T(8,128)} %param.11, bf16[11776,128]{1,0:T(8,128)(2,1)S(1)} %bitcast.67, ...), kind=kOutput, calls=%fused_computation.16 | convolution fusion | flops 1544749056 | bytes 16121856 | tf_op jit(solution)/shard_map/dot_general | solution.py:19
  (1 shorter events, 0.0 us)
Async XLA Ops:
  8.0 26.0 %copy-start = (f32[6,16,512]{2,1,0:T(8,128)S(1)}, f32[6,16,512]{2,1,0:T(8,128)}, u32[]{:S(2)}) copy-start(f32[6,16,512]{2,1,0:T(8,128)} %param.17) | copy-start | bytes 589828
  8.0 190.0 %all-reduce.2.cloned.1.call-start = ((), (), s32[]{:S(2)}) async-start(), calls=%async_computation.1 | async-start | bytes 524288 | tf_op jit(solution)/shard_map/psum | solution.py:64
  8.7 200.1 %all-gather.5.cloned.1.call-start = ((), (), s32[]{:S(2)}) async-start(), calls=%async_computation.2 | async-start | bytes 12247040 | tf_op jit(solution)/shard_map/all_gather | solution.py:42
  15.6 182.4 %copy-start.1 = (f32[1,128,512]{2,1,0:T(8,128)S(1)}, f32[1,128,512]{2,1,0:T(8,128)}, u32[]{:S(2)}) copy-start(f32[1,128,512]{2,1,0:T(8,128)} %param.15) | copy-start | bytes 786436
  15.6 184.9 %all-to-all-start = ((bf16[184,64,128]{2,0,1:T(8,128)(2,1)}), bf16[184,64,128]{2,0,1:T(8,128)(2,1)S(1)}, u32[]{:S(2)}, u32[]{:S(2)}) async-start(bf16[184,64,128]{2,0,1:T(8,128)(2,1)} %copy.16), calls=%async_computation | async-start | bytes 6029312 | tf_op jit(solution)/shard_map/all_to_all | solution.py:41
Sparse Core Ops, SparseCore 0:
  11.8 186.2 all-reduce.1
Sparse Core Ops, SparseCore 1:
  12.5 196.2 all-gather.4
where the time goes:
time: 224 us
  blocking collectives  121 us (54%)
  waiting for transfers between devices  51.8 us (23%)
  starting transfers between devices  17.8 us (8%)
  between operations  16.2 us (7%)
  local copies, waits for them, and re-layouts  7.7 us (3%)
  matrix products  7.24 us (3%)
    all_gather x1, blocking collectives, per_device(): lax.all_gather(momentum.astype(jnp.bfloat16), 'group', axis=0, tiled=True)  95 us
    psum x1, waiting for transfers between devices, per_device(): local_sum = lax.psum(local, 'group')  42.3 us
    all_gather x1, blocking collectives, per_device(): lax.all_gather(anchor.astype(jnp.bfloat16), 'group', axis=0, tiled=True)  25.9 us
    all_to_all x1, starting transfers between devices, per_device(): lax.all_to_all(outgoing, 'fsdp', split_axis=1, concat_axis=0, tiled=True)  17.8 us
    all_gather x1, waiting for transfers between devices, per_device(): lax.all_gather(cotans, 'fsdp', axis=0, tiled=True)  8.3 us
    dot_general x1, matrix products, contract_tokens(): lax.dot_general(features, cotans, (((0,), (0,)), ((), ())), preferred_ele...  7.24 us
  transfers between devices with their start and end apart: 3, of which 2 were waited for; matrix products, arithmetic and copies ran while one was open for 4% of the time, Pallas kernels for 0%

commit v1 on v0

v1 whole, which is shorter than its diff:
```python
import heapq

import jax
import jax.numpy as jnp
from jax import lax
from jax.experimental import pallas as pl
from jax.experimental.pallas import tpu as pltpu
from jax.sharding import PartitionSpec as P

beta_one = 0.9
beta_two = 0.95
bias_one = 1.0 - 0.9**10
bias_two = 1.0 - 0.95**10
inner_rate = 0.01
weight_decay = 0.1
epsilon = 1e-08
outer_rate = 0.7
outer_mu = 0.9
mixing = 0.5

NY, NZ, NC = 8, 4, 2
DYS = (4, 3, -3, 2, -2, 1, -1, 0)
DZS = (2, 1, -1, 0)
UP, DOWN = 0, 1
SIGN = (1, -1)
R1 = 336
H1 = 176
H2 = 96
LANES = 128


def key_order(first):
    order = [(4, dz) for dz in DZS[:first]]
    for dz in DZS:
        order += [(dy, dz) for dy in DYS if (dy, dz) not in order]
    return order


SLOTS = key_order(3)
SLOT = {block: i for i, block in enumerate(SLOTS)}


def schedule():
    link_latency, dot_cost, add_cost = 1.5, 0.16, 0.15
    rate = {"y": 0.050, "z": 0.025}
    size = lambda rows: rows * LANES * 2 / 1e6
    parts1 = (H1, R1 - H1)
    whole2 = 512 - R1
    parts2 = (H2, whole2 - H2)
    steps = {}
    rank = 0

    def add(name, needs, cost, sends, priority):
        steps[name] = (needs, cost, sends, priority)

    for i, block in enumerate(SLOTS):
        add(("dot",) + block, [], dot_cost, [], 3.0 + i * 0.3)
    for s, dz in enumerate(DZS):
        for h in range(NY // 2):
            for d in (UP, DOWN):
                needs = [("dot", 4 if h == 0 else SIGN[d] * (4 - h), dz)]
                if h:
                    needs.append(("y1", s, h - 1, d))
                rows = parts1[d] if h == 0 else R1
                add(("y1", s, h, d), needs, add_cost, [("y", d, size(rows))], s * 1.5 + h)
    both = lambda name, s, h: [(name, s, h, UP), (name, s, h, DOWN)]
    add(("z1", 0, 0), [("dot", 0, 2)] + both("y1", 0, 3), 2 * add_cost,
        [("z", UP, size(parts1[0])), ("z", DOWN, size(parts1[1]))], -2.0)
    for d in (UP, DOWN):
        s = 1 + d
        add(("z1", 1, d), [("dot", 0, DZS[s]), ("z1", 0, 0)] + both("y1", s, 3), 2 * add_cost,
            [("z", d, size(R1))], -2.0)
    add(("z1", 2), [("dot", 0, 0), ("z1", 1, UP), ("z1", 1, DOWN)] + both("y1", 3, 3), 2 * add_cost, [], -2.0)
    for k, dy in enumerate(DYS):
        for h in range(NZ // 2):
            for d in (UP, DOWN):
                needs = [("dot", dy, 2 if h == 0 else SIGN[d])]
                if h:
                    needs.append(("z2", k, 0, d))
                rows = parts2[d] if h == 0 else whole2
                add(("z2", k, h, d), needs, add_cost, [("z", d, size(rows))], k * 0.7 + h * 1.2)
    for h in range(NY // 2):
        for d in (UP, DOWN):
            k = 0 if h == 0 else 2 * h - 1 + d
            needs = [("dot", DYS[k], 0)] + both("z2", k, 1)
            if h:
                needs.append(("y2", h - 1, d))
            rows = parts2[d] if h == 0 else whole2
            add(("y2", h, d), needs, 1.5 * add_cost, [("y", d, size(rows))], -1.0)
    add(("y2", 4), [("dot", 0, 0), ("y2", 3, UP), ("y2", 3, DOWN)] + both("z2", 7, 1), 2 * add_cost, [], -1.0)

    done = {}
    free = {(a, d): 0.0 for a in "yz" for d in (UP, DOWN)}
    now, order = 0.0, []
    left = dict(steps)
    while left:
        best = None
        for name, (needs, cost, sends, priority) in left.items():
            if all(n in done for n in needs):
                ready = max([done[n] for n in needs], default=0.0)
                candidate = (max(ready, now), priority, name)
                if best is None or (candidate[0], candidate[1]) < (best[0], best[1]):
                    best = candidate
        start, _, name = best
        needs, cost, sends, _ = left.pop(name)
        now = start + cost
        done[name] = now
        for axis, d, amount in sends:
            begin = max(free[axis, d], now)
            free[axis, d] = begin + amount / rate[axis]
            done[name] = max(done[name], free[axis, d] + link_latency)
        order.append(name)
    return order, now, free


ORDER = schedule()[0]


def kernel(
    hid, cot, chosen, local, anchor, mom,
    grad_out, local_out, anchor_out, mom_out,
    h_own, h_peer, c_own, c_peer, ct, part, fin,
    y1a, y1b, y1w, z1a, z1b, z1w, z2a, z2b, z2w, y2a, y2b, y2w,
    l_own, l_in, a_all, m_all, a_send, a_in,
    load_sem, peer_send, peer_recv, send_sem, recv_sem, group_send, group_recv,
):
    group = lax.axis_index("group")
    me = lax.axis_index("fsdp")
    groups = lax.axis_size("group")
    y, z, core = me // (NZ * NC), (me // NC) % NZ, me % NC
    place = lambda yy, zz, cc: (lax.rem(yy + NY, NY) * NZ + lax.rem(zz + NZ, NZ)) * NC + cc
    peer = (group, place(y, z, 1 - core))
    partner = {
        "y": [(group, place(y + sign, z, core)) for sign in SIGN],
        "z": [(group, place(y, z + sign, core)) for sign in SIGN],
    }
    members = [(lax.rem(group + r, groups), me) for r in range(1, groups)]
    sublength = anchor.shape[1]

    loads = {}

    def load(name, source, target):
        loads[name] = pltpu.make_async_copy(source, target, load_sem.at[len(loads)])
        loads[name].start()

    def columns(block, cc):
        at = pl.multiple_of(place(y + block[0], z + block[1], cc) * LANES, LANES)
        return hid.at[0, :, pl.ds(at, LANES)]

    load("cot", cot.at[0], c_own)
    for i, block in enumerate(SLOTS):
        load(block, columns(block, core), h_own.at[i])
    load("local", local.at[0], l_own)
    load("anchor", anchor, a_all)
    load("mom", mom, m_all)

    barrier = pltpu.get_barrier_semaphore()
    everyone = [peer] + partner["y"] + partner["z"] + members
    for device in everyone:
        pl.semaphore_signal(barrier, inc=1, device_id=device, device_id_type=pl.DeviceIdType.MESH)
    pl.semaphore_wait(barrier, len(everyone))

    def remote(source, target, send, recv, device):
        return pltpu.make_async_remote_copy(
            src_ref=source, dst_ref=target, send_sem=send, recv_sem=recv,
            device_id=device, device_id_type=pl.DeviceIdType.MESH,
        )

    swaps = [remote(cot.at[0], c_peer, peer_send.at[0], peer_recv.at[0], peer)]
    swaps[0].start()
    for i, block in enumerate(SLOTS):
        swaps.append(
            remote(columns(block, 1 - core), h_peer.at[i], peer_send.at[1 + i], peer_recv.at[1 + i], peer)
        )
        swaps[-1].start()
    spread = []
    for r, device in enumerate(members):
        rows = pl.ds(pl.multiple_of(device[0] * sublength, sublength), sublength)
        spread.append(
            remote(local.at[0, rows], l_in.at[r], group_send.at[r], group_recv.at[r], device)
        )
        spread[-1].start()

    loads["cot"].wait()
    ct[0] = jnp.transpose(c_own[...].astype(jnp.float32)).astype(jnp.bfloat16)
    swaps[0].wait_recv()
    ct[1] = jnp.transpose(c_peer[...].astype(jnp.float32)).astype(jnp.bfloat16)

    messages = {}

    def send(name, axis, d, bufs, index, value):
        number = len(messages)
        out, into = bufs.at[(0,) + index], bufs.at[(1,) + index]
        out[...] = value.astype(jnp.bfloat16)
        messages[name] = (
            remote(out, into, send_sem.at[number], recv_sem.at[number], partner[axis][d]), into,
        )
        messages[name][0].start()

    def arrived(name):
        copy, into = messages[name]
        copy.wait_recv()
        return into[...].astype(jnp.float32)

    def own(dy, dz, begin, end):
        return part[SLOT[dy, dz], begin:end, :]

    def with_part(name, d, whole, cut):
        came = arrived(name)
        if d == UP:
            return jnp.concatenate([whole[:cut] + came, whole[cut:]], axis=0)
        return jnp.concatenate([whole[:cut], whole[cut:] + came], axis=0)

    def step_dot(dy, dz):
        i = SLOT[dy, dz]
        loads[dy, dz].wait()
        swaps[1 + i].wait_recv()
        part[i] = jnp.dot(ct[0], h_own[i], preferred_element_type=jnp.float32) + jnp.dot(
            ct[1], h_peer[i], preferred_element_type=jnp.float32
        )

    def step_y1(s, h, d):
        dz = DZS[s]
        if h == 0:
            begin, end = ((0, H1), (H1, R1))[d]
            send(("y1", s, h, d), "y", d, (y1a, y1b)[d], (s,), own(4, dz, begin, end))
            return
        whole = own(SIGN[d] * (4 - h), dz, 0, R1)
        if h == 1:
            whole = with_part(("y1", s, 0, d), d, whole, H1)
        else:
            whole = whole + arrived(("y1", s, h - 1, d))
        send(("y1", s, h, d), "y", d, y1w, (d, h - 1, s), whole)

    def y1_sum(s):
        return own(0, DZS[s], 0, R1) + arrived(("y1", s, 3, UP)) + arrived(("y1", s, 3, DOWN))

    def step_z1(h, d=None):
        if h == 0:
            whole = y1_sum(0)
            send(("z1", 0, UP), "z", UP, z1a, (), whole[:H1])
            send(("z1", 0, DOWN), "z", DOWN, z1b, (), whole[H1:])
        elif h == 1:
            whole = with_part(("z1", 0, d), d, y1_sum(1 + d), H1)
            send(("z1", 1, d), "z", d, z1w, (d,), whole)
        else:
            fin[0:R1, :] = y1_sum(3) + arrived(("z1", 1, UP)) + arrived(("z1", 1, DOWN))

    def step_z2(k, h, d):
        dy = DYS[k]
        if h == 0:
            begin, end = ((R1, R1 + H2), (R1 + H2, 512))[d]
            send(("z2", k, h, d), "z", d, (z2a, z2b)[d], (k,), own(dy, 2, begin, end))
            return
        whole = with_part(("z2", k, 0, d), d, own(dy, SIGN[d], R1, 512), H2)
        send(("z2", k, h, d), "z", d, z2w, (d, k), whole)

    def z2_sum(k):
        return own(DYS[k], 0, R1, 512) + arrived(("z2", k, 1, UP)) + arrived(("z2", k, 1, DOWN))

    far = []

    def step_y2(h, d=None):
        if h == 0:
            if not far:
                far.append(z2_sum(0))
            value = far[0][:H2] if d == UP else far[0][H2:]
            send(("y2", 0, d), "y", d, (y2a, y2b)[d], (), value)
        elif h < 4:
            whole = z2_sum(2 * h - 1 + d)
            if h == 1:
                whole = with_part(("y2", 0, d), d, whole, H2)
            else:
                whole = whole + arrived(("y2", h - 1, d))
            send(("y2", h, d), "y", d, y2w, (d, h - 1), whole)
        else:
            fin[R1:512, :] = z2_sum(7) + arrived(("y2", 3, UP)) + arrived(("y2", 3, DOWN))

    returned = []

    def outer_first():
        for name in ("local", "anchor", "mom"):
            loads[name].wait()
        at = pl.multiple_of(group * sublength, sublength)
        total = l_own[pl.ds(at, sublength), :]
        for r, copy in enumerate(spread):
            copy.wait_recv()
            total = total + l_in[r]
        f = chosen[0]
        here = a_all[f]
        mean_delta = here - total * (1.0 / groups)
        momentum_next = outer_mu * m_all[f] + mean_delta
        anchor_next = here - outer_rate * (mean_delta + outer_mu * momentum_next)
        anchor_out[...] = anchor_next
        mom_out[...] = momentum_next
        a_send[...] = anchor_next.astype(jnp.bfloat16)
        for r, device in enumerate(members):
            returned.append(
                remote(a_send, a_in.at[r], group_send.at[groups - 1 + r], group_recv.at[groups - 1 + r], device)
            )
            returned[-1].start()
        rows = pl.ds(at, sublength)
        local_out[rows, :] = mixing * l_own[rows, :] + (1.0 - mixing) * anchor_next

    def outer_second():
        for r, copy in enumerate(returned):
            copy.wait_recv()
            source = lax.rem(group + groups - 1 - r, groups)
            rows = pl.ds(pl.multiple_of(source * sublength, sublength), sublength)
            local_out[rows, :] = mixing * l_own[rows, :] + (1.0 - mixing) * a_in[r].astype(jnp.float32)

    run = {"dot": step_dot, "y1": step_y1, "z1": step_z1, "z2": step_z2, "y2": step_y2}
    for number, name in enumerate(ORDER):
        if number == len(ORDER) // 2:
            outer_first()
        if number == len(ORDER) * 3 // 4:
            outer_second()
        run[name[0]](*name[1:])

    grad_out[...] = jnp.transpose(fin[...])
    for copy in swaps + spread + returned + [copy for copy, _ in messages.values()]:
        copy.wait_send()


def reduced(hidden, cotangent, sync_frag, frag_local, frag_anchor, frag_momentum):
    tokens, keys = cotangent.shape[1:]
    frags, sublength, _ = frag_anchor.shape
    rows = frag_local.shape[1]
    groups = lax.axis_size("group")
    blocks = len(SLOTS)
    bf16, f32 = jnp.bfloat16, jnp.float32
    half1, half2 = (H1, R1 - H1), (H2, keys - R1 - H2)
    n1, n2 = R1, keys - R1
    messages = 2 * (16 + 2 + 16 + 4)
    vmem = pl.BlockSpec(memory_space=pltpu.VMEM)
    hbm = pl.BlockSpec(memory_space=pl.ANY)
    return pl.pallas_call(
        kernel,
        out_shape=(
            jax.ShapeDtypeStruct((rows, keys), f32),
            jax.ShapeDtypeStruct((rows, keys), f32),
            jax.ShapeDtypeStruct((sublength, keys), f32),
            jax.ShapeDtypeStruct((sublength, keys), f32),
        ),
        in_specs=[hbm, hbm, pl.BlockSpec(memory_space=pltpu.SMEM), hbm, hbm, hbm],
        out_specs=(vmem, vmem, vmem, vmem),
        scratch_shapes=[
            pltpu.VMEM((blocks, tokens, LANES), bf16),
            pltpu.VMEM((blocks, tokens, LANES), bf16),
            pltpu.VMEM((tokens, keys), bf16),
            pltpu.VMEM((tokens, keys), bf16),
            pltpu.VMEM((2, keys, tokens), bf16),
            pltpu.VMEM((blocks, keys, LANES), f32),
            pltpu.VMEM((keys, LANES), f32),
            pltpu.VMEM((2, NZ, half1[0], LANES), bf16),
            pltpu.VMEM((2, NZ, half1[1], LANES), bf16),
            pltpu.VMEM((2, 2, NY // 2 - 1, NZ, n1, LANES), bf16),
            pltpu.VMEM((2, half1[0], LANES), bf16),
            pltpu.VMEM((2, half1[1], LANES), bf16),
            pltpu.VMEM((2, 2, n1, LANES), bf16),
            pltpu.VMEM((2, NY, half2[0], LANES), bf16),
            pltpu.VMEM((2, NY, half2[1], LANES), bf16),
            pltpu.VMEM((2, 2, NY, n2, LANES), bf16),
            pltpu.VMEM((2, half2[0], LANES), bf16),
            pltpu.VMEM((2, half2[1], LANES), bf16),
            pltpu.VMEM((2, 2, NY // 2 - 1, n2, LANES), bf16),
            pltpu.VMEM((rows, keys), f32),
            pltpu.VMEM((groups - 1, sublength, keys), f32),
            pltpu.VMEM((frags, sublength, keys), f32),
            pltpu.VMEM((frags, sublength, keys), f32),
            pltpu.VMEM((sublength, keys), bf16),
            pltpu.VMEM((groups - 1, sublength, keys), bf16),
            pltpu.SemaphoreType.DMA((blocks + 4,)),
            pltpu.SemaphoreType.DMA((blocks + 1,)),
            pltpu.SemaphoreType.DMA((blocks + 1,)),
            pltpu.SemaphoreType.DMA((messages,)),
            pltpu.SemaphoreType.DMA((messages,)),
            pltpu.SemaphoreType.DMA((2 * (groups - 1),)),
            pltpu.SemaphoreType.DMA((2 * (groups - 1),)),
        ],
        compiler_params=pltpu.CompilerParams(
            collective_id=0, has_side_effects=True, vmem_limit_bytes=40 * 1024 * 1024
        ),
        name="reduce_and_sync",
    )(hidden, cotangent, sync_frag, frag_local, frag_anchor, frag_momentum)


def per_device(
    hidden,
    cotangent,
    weight,
    first_moment,
    second_moment,
    sync_frag,
    frag_local,
    frag_anchor,
    frag_momentum,
):
    gradient, new_local, anchor_out, momentum_out = reduced(
        hidden, cotangent, sync_frag, frag_local, frag_anchor, frag_momentum
    )
    moment_one = beta_one * first_moment[0].astype(jnp.float32) + (1.0 - beta_one) * gradient
    moment_two = (
        beta_two * second_moment[0].astype(jnp.float32) + (1.0 - beta_two) * gradient * gradient
    )
    step_size = moment_one / bias_one / (jnp.sqrt(moment_two / bias_two) + epsilon)
    master = weight[0]
    new_weight = master - inner_rate * (step_size + weight_decay * master)
    return (
        new_weight[None],
        moment_one.astype(jnp.bfloat16)[None],
        moment_two.astype(jnp.bfloat16)[None],
        new_local[None],
        anchor_out,
        momentum_out,
    )


def solution(mesh):
    in_specs = (
        P("group", "fsdp", None),
        P("group", "fsdp", None),
        P("group", "fsdp", None),
        P("group", "fsdp", None),
        P("group", "fsdp", None),
        P(),
        P("group", "fsdp", None),
        P(None, ("fsdp", "group"), None),
        P(None, ("fsdp", "group"), None),
    )
    out_specs = (
        P("group", "fsdp", None),
        P("group", "fsdp", None),
        P("group", "fsdp", None),
        P("group", "fsdp", None),
        P(("fsdp", "group"), None),
        P(("fsdp", "group"), None),
    )
    return jax.shard_map(
        per_device, mesh=mesh, in_specs=in_specs, out_specs=out_specs, check_vma=False
    )
```

time: 224 us -> 73 us (0.33)
  the two profiles are of different devices: /device:TPU:1 before, /device:TPU:8 now
where the time goes in v1:
time: 73 us; the launch traced here: 72.7 us
  Pallas kernels  62.8 us (86%)
  local copies, waits for them, and re-layouts  7.51 us (10%)
  between operations  1.33 us (2%)
  other arithmetic  1.08 us (1%)
    pallas_call x1, Pallas kernels, reduced(): pl.pallas_call(kernel, out_shape=(jax.ShapeDtypeStruct((rows, keys), f32)...  62.8 us
    unnamed x19, local copies, waits for them, and re-layouts  7.51 us

profile of v1, /device:TPU:8, one launch (start us, length us, event | category | flops | bytes accessed | tf_op | source)
XLA Modules:
  0.0 72.7 jit_solution(7950315718175989272)
XLA Ops:
  1.3 0.0 copy-start
  1.3 1.8 %copy-done = bf16[1,184,8192]{2,1,0:T(8,128)(2,1)S(1)} copy-done((bf16[1,184,8192]{2,1,0:T(8,128)(2,1)S(1)}, bf16[1,184,8192]{2,1,0:T(8,128)(2,1)}, u32[]{:S(2)}) %copy-start) | copy-done | bytes 3014680
  3.1 0.0 copy-start.1
  3.1 0.9 %copy-done.1 = f32[1,128,512]{2,1,0:T(8,128)S(1)} copy-done((f32[1,128,512]{2,1,0:T(8,128)S(1)}, f32[1,128,512]{2,1,0:T(8,128)}, u32[]{:S(2)}) %copy-start.1) | copy-done | bytes 262168
  4.1 0.0 copy-start.2
  4.1 0.9 %copy-done.2 = f32[6,16,512]{2,1,0:T(8,128)S(1)} copy-done((f32[6,16,512]{2,1,0:T(8,128)S(1)}, f32[6,16,512]{2,1,0:T(8,128)}, u32[]{:S(2)}) %copy-start.2) | copy-done | bytes 196632
  5.0 0.0 copy-start.3
  5.0 0.9 %copy-done.3 = f32[6,16,512]{2,1,0:T(8,128)S(1)} copy-done((f32[6,16,512]{2,1,0:T(8,128)S(1)}, f32[6,16,512]{2,1,0:T(8,128)}, u32[]{:S(2)}) %copy-start.3) | copy-done | bytes 196632
  5.9 0.0 copy-start.4
  5.9 0.9 %copy-done.4 = bf16[1,184,512]{2,1,0:T(8,128)(2,1)S(1)} copy-done((bf16[1,184,512]{2,1,0:T(8,128)(2,1)S(1)}, bf16[1,184,512]{2,1,0:T(8,128)(2,1)}, u32[]{:S(2)}) %copy-start.4) | copy-done | bytes 188440
  6.9 0.0 copy-start.5
  6.9 0.0 copy-start.6
  6.9 0.0 copy-start.7
  6.9 62.8 %reduce_and_sync.1 = (f32[128,512]{1,0:T(8,128)S(1)}, f32[128,512]{1,0:T(8,128)S(1)}, f32[16,512]{1,0:T(8,128)S(1)}, f32[16,512]{1,0:T(8,128)S(1)}) custom-call(bf16[1,184,8192]{2,1,0:T(8,128)(2,1)S(1)} %copy-done, bf16[1,184,512]{2,1,0:T(8,128)(2,1)S(1)} %copy-done.4, s32[1]{0:T(128)S(6)} %copy.18.chosen, f32[1,128,512]{2,1,0:T(8,128)S(1)} %copy-done.1, ...), custom_call_target="tpu_custom_call" | custom-call | tf_op jit(solution)/shard_map/reduce_and_sync/pallas_call | solution.py:337
  69.7 0.0 copy-done.5
  69.7 0.0 copy-done.6
  69.7 0.0 copy-done.7
  69.7 1.1 %fusion.6 = (bf16[1,128,512]{2,1,0:T(8,128)(2,1)}, f32[1,128,512]{2,1,0:T(8,128)}, bf16[1,128,512]{2,1,0:T(8,128)(2,1)}) fusion(f32[128,512]{1,0:T(8,128)S(1)} %get-tuple-element.10, bf16[1,128,512]{2,1,0:T(8,128)(2,1)S(1)} %copy-done.6, bf16[1,128,512]{2,1,0:T(8,128)(2,1)S(1)} %copy-done.7, f32[1,128,512]{2,1,0:T(8,128)S(1)} %copy-done.5), kind=kLoop, calls=%fused_computation.10 | loop fusion | flops 1245184 | bytes 1310720 | tf_op jit(solution)/shard_map/broadcast_in_dim | solution.py:412
  70.8 0.7 copy.19
  71.5 0.6 copy.20
  72.1 0.6 copy.21
Async XLA Ops:
  1.3 1.9 %copy-start = (bf16[1,184,8192]{2,1,0:T(8,128)(2,1)S(1)}, bf16[1,184,8192]{2,1,0:T(8,128)(2,1)}, u32[]{:S(2)}) copy-start(bf16[1,184,8192]{2,1,0:T(8,128)(2,1)} %hid.1) | copy-start | bytes 9043972
  3.1 0.9 %copy-start.1 = (f32[1,128,512]{2,1,0:T(8,128)S(1)}, f32[1,128,512]{2,1,0:T(8,128)}, u32[]{:S(2)}) copy-start(f32[1,128,512]{2,1,0:T(8,128)} %local.1) | copy-start | bytes 786436
  4.1 0.9 %copy-start.2 = (f32[6,16,512]{2,1,0:T(8,128)S(1)}, f32[6,16,512]{2,1,0:T(8,128)}, u32[]{:S(2)}) copy-start(f32[6,16,512]{2,1,0:T(8,128)} %anchor.1) | copy-start | bytes 589828
  5.0 0.9 %copy-start.3 = (f32[6,16,512]{2,1,0:T(8,128)S(1)}, f32[6,16,512]{2,1,0:T(8,128)}, u32[]{:S(2)}) copy-start(f32[6,16,512]{2,1,0:T(8,128)} %mom.1) | copy-start | bytes 589828
  5.9 0.9 %copy-start.4 = (bf16[1,184,512]{2,1,0:T(8,128)(2,1)S(1)}, bf16[1,184,512]{2,1,0:T(8,128)(2,1)}, u32[]{:S(2)}) copy-start(bf16[1,184,512]{2,1,0:T(8,128)(2,1)} %cot.1) | copy-start | bytes 565252
  6.9 62.8 %copy-start.5 = (f32[1,128,512]{2,1,0:T(8,128)S(1)}, f32[1,128,512]{2,1,0:T(8,128)}, u32[]{:S(2)}) copy-start(f32[1,128,512]{2,1,0:T(8,128)} %param.11) | copy-start | bytes 786436
  6.9 62.8 %copy-start.6 = (bf16[1,128,512]{2,1,0:T(8,128)(2,1)S(1)}, bf16[1,128,512]{2,1,0:T(8,128)(2,1)}, u32[]{:S(2)}) copy-start(bf16[1,128,512]{2,1,0:T(8,128)(2,1)} %param.13) | copy-start | bytes 393220
  6.9 62.8 %copy-start.7 = (bf16[1,128,512]{2,1,0:T(8,128)(2,1)S(1)}, bf16[1,128,512]{2,1,0:T(8,128)(2,1)}, u32[]{:S(2)}) copy-start(bf16[1,128,512]{2,1,0:T(8,128)(2,1)} %param.12) | copy-start | bytes 393220

commit v2 on v1

--- a/solution.py
+++ b/solution.py
@@ -1,5 +1,3 @@
-import heapq
-
 import jax
 import jax.numpy as jnp
 from jax import lax
@@ -23,98 +21,39 @@
 DZS = (2, 1, -1, 0)
 UP, DOWN = 0, 1
 SIGN = (1, -1)
-R1 = 336
+R1 = 352
 H1 = 176
-H2 = 96
+H2 = 80
 LANES = 128
 
 
-def key_order(first):
-    order = [(4, dz) for dz in DZS[:first]]
-    for dz in DZS:
-        order += [(dy, dz) for dy in DYS if (dy, dz) not in order]
-    return order
-
-
-SLOTS = key_order(3)
-SLOT = {block: i for i, block in enumerate(SLOTS)}
-
-
-def schedule():
-    link_latency, dot_cost, add_cost = 1.5, 0.16, 0.15
-    rate = {"y": 0.050, "z": 0.025}
-    size = lambda rows: rows * LANES * 2 / 1e6
-    parts1 = (H1, R1 - H1)
-    whole2 = 512 - R1
-    parts2 = (H2, whole2 - H2)
-    steps = {}
-    rank = 0
-
-    def add(name, needs, cost, sends, priority):
-        steps[name] = (needs, cost, sends, priority)
-
-    for i, block in enumerate(SLOTS):
-        add(("dot",) + block, [], dot_cost, [], 3.0 + i * 0.3)
-    for s, dz in enumerate(DZS):
-        for h in range(NY // 2):
-            for d in (UP, DOWN):
-                needs = [("dot", 4 if h == 0 else SIGN[d] * (4 - h), dz)]
-                if h:
-                    needs.append(("y1", s, h - 1, d))
-                rows = parts1[d] if h == 0 else R1
-                add(("y1", s, h, d), needs, add_cost, [("y", d, size(rows))], s * 1.5 + h)
-    both = lambda name, s, h: [(name, s, h, UP), (name, s, h, DOWN)]
-    add(("z1", 0, 0), [("dot", 0, 2)] + both("y1", 0, 3), 2 * add_cost,
-        [("z", UP, size(parts1[0])), ("z", DOWN, size(parts1[1]))], -2.0)
-    for d in (UP, DOWN):
-        s = 1 + d
-        add(("z1", 1, d), [("dot", 0, DZS[s]), ("z1", 0, 0)] + both("y1", s, 3), 2 * add_cost,
-            [("z", d, size(R1))], -2.0)
-    add(("z1", 2), [("dot", 0, 0), ("z1", 1, UP), ("z1", 1, DOWN)] + both("y1", 3, 3), 2 * add_cost, [], -2.0)
-    for k, dy in enumerate(DYS):
-        for h in range(NZ // 2):
-            for d in (UP, DOWN):
-                needs = [("dot", dy, 2 if h == 0 else SIGN[d])]
-                if h:
-                    needs.append(("z2", k, 0, d))
-                rows = parts2[d] if h == 0 else whole2
-                add(("z2", k, h, d), needs, add_cost, [("z", d, size(rows))], k * 0.7 + h * 1.2)
-    for h in range(NY // 2):
-        for d in (UP, DOWN):
-            k = 0 if h == 0 else 2 * h - 1 + d
-            needs = [("dot", DYS[k], 0)] + both("z2", k, 1)
-            if h:
-                needs.append(("y2", h - 1, d))
-            rows = parts2[d] if h == 0 else whole2
-            add(("y2", h, d), needs, 1.5 * add_cost, [("y", d, size(rows))], -1.0)
-    add(("y2", 4), [("dot", 0, 0), ("y2", 3, UP), ("y2", 3, DOWN)] + both("z2", 7, 1), 2 * add_cost, [], -1.0)
-
-    done = {}
-    free = {(a, d): 0.0 for a in "yz" for d in (UP, DOWN)}
-    now, order = 0.0, []
-    left = dict(steps)
-    while left:
-        best = None
-        for name, (needs, cost, sends, priority) in left.items():
-            if all(n in done for n in needs):
-                ready = max([done[n] for n in needs], default=0.0)
-                candidate = (max(ready, now), priority, name)
-                if best is None or (candidate[0], candidate[1]) < (best[0], best[1]):
-                    best = candidate
-        start, _, name = best
-        needs, cost, sends, _ = left.pop(name)
-        now = start + cost
-        done[name] = now
-        for axis, d, amount in sends:
-            begin = max(free[axis, d], now)
-            free[axis, d] = begin + amount / rate[axis]
-            done[name] = max(done[name], free[axis, d] + link_latency)
-        order.append(name)
-    return order, now, free
-
-
-ORDER = schedule()[0]
-
+PAIRS = (
+    (((4, 2), (4, 1)), ((4, -1), (4, 0)))
+    + tuple(((dy, 2), (-dy, 2)) for dy in (3, 2, 1))
+    + (((0, 2), (0, 0)),)
+    + tuple(((dy, 1), (dy, -1)) for dy in (3, -3, 2, -2, 1, -1, 0))
+    + tuple(((dy, 0), (-dy, 0)) for dy in (3, 2, 1))
+)
+SLOT = {block: (i, j) for i, pair in enumerate(PAIRS) for j, block in enumerate(pair)}
+
+ORDER = (
+    ("dot", 0), ("y1", 0, 0, 0), ("y1", 0, 0, 1), ("z2", 0, 0, 1), ("z2", 0, 0, 0), ("y1", 1, 0, 1),
+    ("y1", 1, 0, 0), ("dot", 3), ("z2", 3, 0, 1), ("z2", 4, 0, 0), ("z2", 3, 0, 0), ("dot", 1),
+    ("y1", 3, 0, 0), ("z2", 4, 0, 1), ("y1", 2, 0, 1), ("y1", 3, 0, 1), ("y1", 2, 0, 0), ("dot", 2),
+    ("dot", 4), ("z2", 5, 0, 1), ("z2", 1, 0, 0), ("dot", 6), ("z2", 2, 0, 1), ("y1", 0, 1, 0),
+    ("y1", 0, 1, 1), ("dot", 7), ("z2", 2, 0, 0), ("dot", 5), ("z2", 6, 0, 0), ("z2", 1, 0, 1),
+    ("z2", 0, 1, 1), ("y1", 1, 1, 1), ("y1", 1, 1, 0), ("dot", 15), ("z2", 5, 0, 0), ("dot", 10),
+    ("z2", 6, 0, 1), ("y1", 2, 1, 0), ("y1", 2, 1, 1), ("z2", 7, 0, 1), ("z2", 0, 1, 0), ("dot", 14),
+    ("dot", 8), ("z2", 7, 0, 0), ("dot", 9), ("y1", 0, 2, 1), ("z2", 2, 1, 1), ("y1", 0, 2, 0),
+    ("z2", 1, 1, 0), ("z2", 4, 1, 1), ("dot", 12), ("y1", 1, 2, 0), ("z2", 4, 1, 0), ("z2", 3, 1, 1),
+    ("y1", 1, 2, 1), ("y1", 2, 2, 0), ("z2", 2, 1, 0), ("y1", 2, 2, 1), ("z2", 7, 1, 1), ("y1", 0, 3, 1),
+    ("y1", 0, 3, 0), ("dot", 13), ("y2", 0, 1), ("y2", 0, 0), ("z2", 1, 1, 1), ("dot", 11), ("z2", 5, 1, 0),
+    ("z2", 3, 1, 0), ("y1", 1, 3, 0), ("y1", 3, 1, 1), ("y1", 1, 3, 1), ("y1", 3, 1, 0), ("z1", 0, 0),
+    ("y1", 2, 3, 1), ("y1", 2, 3, 0), ("z2", 5, 1, 1), ("z2", 6, 1, 1), ("z2", 7, 1, 0), ("y2", 1, 1),
+    ("y2", 1, 0), ("y1", 3, 2, 1), ("z2", 6, 1, 0), ("y1", 3, 2, 0), ("z1", 1, 0), ("z1", 1, 1),
+    ("y2", 2, 0), ("y2", 2, 1), ("y1", 3, 3, 0), ("y1", 3, 3, 1), ("y2", 3, 0), ("y2", 3, 1), ("z1", 2),
+    ("y2", 4),
+)
 
 def kernel(
     hid, cot, chosen, local, anchor, mom,
@@ -137,27 +76,31 @@
     members = [(lax.rem(group + r, groups), me) for r in range(1, groups)]
     sublength = anchor.shape[1]
 
-    loads = {}
-
-    def load(name, source, target):
-        loads[name] = pltpu.make_async_copy(source, target, load_sem.at[len(loads)])
-        loads[name].start()
-
-    def columns(block, cc):
-        at = pl.multiple_of(place(y + block[0], z + block[1], cc) * LANES, LANES)
-        return hid.at[0, :, pl.ds(at, LANES)]
-
-    load("cot", cot.at[0], c_own)
-    for i, block in enumerate(SLOTS):
-        load(block, columns(block, core), h_own.at[i])
-    load("local", local.at[0], l_own)
-    load("anchor", anchor, a_all)
-    load("mom", mom, m_all)
-
     barrier = pltpu.get_barrier_semaphore()
     everyone = [peer] + partner["y"] + partner["z"] + members
     for device in everyone:
         pl.semaphore_signal(barrier, inc=1, device_id=device, device_id_type=pl.DeviceIdType.MESH)
+
+    loads = {}
+
+    def load(name, source, target):
+        loads[name] = pltpu.make_async_copy(source, target, load_sem.at[len(loads)])
+        loads[name].start()
+
+    def columns(block, cc):
+        at = pl.multiple_of(place(y + block[0], z + block[1], cc) * LANES, LANES)
+        return hid.at[0, :, pl.ds(at, LANES)]
+
+    def half(ref, block):
+        i, j = SLOT[block]
+        return ref.at[i, :, j * LANES : (j + 1) * LANES]
+
+    load("cot", cot.at[0], c_own)
+    for block in SLOT:
+        load(block, columns(block, core), half(h_own, block))
+    load("local", local.at[0], l_own)
+    load("anchor", anchor, a_all)
+    load("mom", mom, m_all)
     pl.semaphore_wait(barrier, len(everyone))
 
     def remote(source, target, send, recv, device):
@@ -166,13 +109,13 @@
             device_id=device, device_id_type=pl.DeviceIdType.MESH,
         )
 
-    swaps = [remote(cot.at[0], c_peer, peer_send.at[0], peer_recv.at[0], peer)]
-    swaps[0].start()
-    for i, block in enumerate(SLOTS):
-        swaps.append(
-            remote(columns(block, 1 - core), h_peer.at[i], peer_send.at[1 + i], peer_recv.at[1 + i], peer)
+    swaps = {"cot": remote(cot.at[0], c_peer, peer_send.at[0], peer_recv.at[0], peer)}
+    swaps["cot"].start()
+    for i, block in enumerate(SLOT, 1):
+        swaps[block] = remote(
+            columns(block, 1 - core), half(h_peer, block), peer_send.at[i], peer_recv.at[i], peer
         )
-        swaps[-1].start()
+        swaps[block].start()
     spread = []
     for r, device in enumerate(members):
         rows = pl.ds(pl.multiple_of(device[0] * sublength, sublength), sublength)
@@ -183,7 +126,7 @@
 
     loads["cot"].wait()
     ct[0] = jnp.transpose(c_own[...].astype(jnp.float32)).astype(jnp.bfloat16)
-    swaps[0].wait_recv()
+    swaps["cot"].wait_recv()
     ct[1] = jnp.transpose(c_peer[...].astype(jnp.float32)).astype(jnp.bfloat16)
 
     messages = {}
@@ -203,7 +146,8 @@
         return into[...].astype(jnp.float32)
 
     def own(dy, dz, begin, end):
-        return part[SLOT[dy, dz], begin:end, :]
+        i, j = SLOT[dy, dz]
+        return part[i, begin:end, j * LANES : (j + 1) * LANES]
 
     def with_part(name, d, whole, cut):
         came = arrived(name)
@@ -211,10 +155,10 @@
             return jnp.concatenate([whole[:cut] + came, whole[cut:]], axis=0)
         return jnp.concatenate([whole[:cut], whole[cut:] + came], axis=0)
 
-    def step_dot(dy, dz):
-        i = SLOT[dy, dz]
-        loads[dy, dz].wait()
-        swaps[1 + i].wait_recv()
+    def step_dot(i):
+        for block in PAIRS[i]:
+            loads[block].wait()
+            swaps[block].wait_recv()
         part[i] = jnp.dot(ct[0], h_own[i], preferred_element_type=jnp.float32) + jnp.dot(
             ct[1], h_peer[i], preferred_element_type=jnp.float32
         )
@@ -318,7 +262,7 @@
         run[name[0]](*name[1:])
 
     grad_out[...] = jnp.transpose(fin[...])
-    for copy in swaps + spread + returned + [copy for copy, _ in messages.values()]:
+    for copy in list(swaps.values()) + spread + returned + [copy for copy, _ in messages.values()]:
         copy.wait_send()
 
 
@@ -327,13 +271,14 @@
     frags, sublength, _ = frag_anchor.shape
     rows = frag_local.shape[1]
     groups = lax.axis_size("group")
-    blocks = len(SLOTS)
+    pairs, blocks = len(PAIRS), len(SLOT)
     bf16, f32 = jnp.bfloat16, jnp.float32
     half1, half2 = (H1, R1 - H1), (H2, keys - R1 - H2)
     n1, n2 = R1, keys - R1
     messages = 2 * (16 + 2 + 16 + 4)
     vmem = pl.BlockSpec(memory_space=pltpu.VMEM)
-    hbm = pl.BlockSpec(memory_space=pl.ANY)
+    hbm = pl.BlockSpec(memory_space=pltpu.HBM)
+    stay = lambda x: pltpu.with_memory_space_constraint(x, pltpu.HBM)
     return pl.pallas_call(
         kernel,
         out_shape=(
@@ -345,12 +290,12 @@
         in_specs=[hbm, hbm, pl.BlockSpec(memory_space=pltpu.SMEM), hbm, hbm, hbm],
         out_specs=(vmem, vmem, vmem, vmem),
         scratch_shapes=[
-            pltpu.VMEM((blocks, tokens, LANES), bf16),
-            pltpu.VMEM((blocks, tokens, LANES), bf16),
+            pltpu.VMEM((pairs, tokens, 2 * LANES), bf16),
+            pltpu.VMEM((pairs, tokens, 2 * LANES), bf16),
             pltpu.VMEM((tokens, keys), bf16),
             pltpu.VMEM((tokens, keys), bf16),
             pltpu.VMEM((2, keys, tokens), bf16),
-            pltpu.VMEM((blocks, keys, LANES), f32),
+            pltpu.VMEM((pairs, keys, 2 * LANES), f32),
             pltpu.VMEM((keys, LANES), f32),
             pltpu.VMEM((2, NZ, half1[0], LANES), bf16),
             pltpu.VMEM((2, NZ, half1[1], LANES), bf16),
@@ -382,7 +327,44 @@
             collective_id=0, has_side_effects=True, vmem_limit_bytes=40 * 1024 * 1024
         ),
         name="reduce_and_sync",
-    )(hidden, cotangent, sync_frag, frag_local, frag_anchor, frag_momentum)
+    )(stay(hidden), stay(cotangent), sync_frag, stay(frag_local), stay(frag_anchor), stay(frag_momentum))
+
+
+def finish(
+    gradient, weight, first, second, local, anchor, momentum,
+    weight_out, first_out, second_out, local_out, anchor_out, momentum_out,
+):
+    slope = gradient[...]
+    moment_one = beta_one * first[0].astype(jnp.float32) + (1.0 - beta_one) * slope
+    moment_two = beta_two * second[0].astype(jnp.float32) + (1.0 - beta_two) * slope * slope
+    step_size = moment_one / bias_one / (jnp.sqrt(moment_two / bias_two) + epsilon)
+    master = weight[0]
+    weight_out[0] = master - inner_rate * (step_size + weight_decay * master)
+    first_out[0] = moment_one.astype(jnp.bfloat16)
+    second_out[0] = moment_two.astype(jnp.bfloat16)
+    local_out[0] = local[...]
+    anchor_out[...] = anchor[...]
+    momentum_out[...] = momentum[...]
+
+
+def finished(gradient, weight, first, second, local, anchor, momentum):
+    vmem = pl.BlockSpec(memory_space=pltpu.VMEM)
+    shape = jax.ShapeDtypeStruct
+    return pl.pallas_call(
+        finish,
+        out_shape=(
+            shape(weight.shape, weight.dtype),
+            shape(first.shape, first.dtype),
+            shape(second.shape, second.dtype),
+            shape(weight.shape, local.dtype),
+            shape(anchor.shape, anchor.dtype),
+            shape(momentum.shape, momentum.dtype),
+        ),
+        in_specs=[vmem] * 7,
+        out_specs=(vmem,) * 6,
+        compiler_params=pltpu.CompilerParams(vmem_limit_bytes=16 * 1024 * 1024),
+        name="finish",
+    )(gradient, weight, first, second, local, anchor, momentum)
 
 
 def per_device(
@@ -399,20 +381,8 @@
     gradient, new_local, anchor_out, momentum_out = reduced(
         hidden, cotangent, sync_frag, frag_local, frag_anchor, frag_momentum
     )
-    moment_one = beta_one * first_moment[0].astype(jnp.float32) + (1.0 - beta_one) * gradient
-    moment_two = (
-        beta_two * second_moment[0].astype(jnp.float32) + (1.0 - beta_two) * gradient * gradient
-    )
-    step_size = moment_one / bias_one / (jnp.sqrt(moment_two / bias_two) + epsilon)
-    master = weight[0]
-    new_weight = master - inner_rate * (step_size + weight_decay * master)
-    return (
-        new_weight[None],
-        moment_one.astype(jnp.bfloat16)[None],
-        moment_two.astype(jnp.bfloat16)[None],
-        new_local[None],
-        anchor_out,
-        momentum_out,
+    return finished(
+        gradient, weight, first_moment, second_moment, new_local, anchor_out, momentum_out
     )
 
 

time: 73 us -> 56.3 us (0.77)
  the two profiles are of different devices: /device:TPU:8 before, /device:TPU:66 now
where the time goes in v2:
time: 56.3 us; the launch traced here: 56.2 us
  Pallas kernels  54.8 us (97%)
  between operations  1.39 us (2%)
    pallas_call x1, Pallas kernels, reduced(): pl.pallas_call(kernel, out_shape=(jax.ShapeDtypeStruct((rows, keys), f32)...  53.8 us

profile of v2, /device:TPU:66, one launch (start us, length us, event | category | flops | bytes accessed | tf_op | source)
XLA Modules:
  0.0 56.2 jit_solution(2242563337347512246)
XLA Ops:
  0.6 0.0 copy-start.2
  0.6 0.0 copy-start.1
  0.7 0.0 copy-start
  1.4 53.8 %reduce_and_sync.1 = (f32[128,512]{1,0:T(8,128)S(1)}, f32[128,512]{1,0:T(8,128)S(1)}, f32[16,512]{1,0:T(8,128)S(1)}, f32[16,512]{1,0:T(8,128)S(1)}) custom-call(bf16[1,184,8192]{2,1,0:T(8,128)(2,1)} %hid.1, bf16[1,184,512]{2,1,0:T(8,128)(2,1)} %cot.1, s32[1]{0:T(128)S(6)} %copy.15.chosen, f32[1,128,512]{2,1,0:T(8,128)} %local.1, f32[6,16,512]{2,1,0:T(8,128)} %anchor.1, ...), custom_call_target="tpu_custom_call" | custom-call | tf_op jit(solution)/shard_map/reduce_and_sync/pallas_call | solution.py:282
  55.1 0.0 copy-done.2
  55.1 0.0 copy-done.1
  55.1 0.0 copy-done
  55.2 1.0 %finish.1 = (f32[1,128,512]{2,1,0:T(8,128)}, bf16[1,128,512]{2,1,0:T(8,128)(2,1)}, bf16[1,128,512]{2,1,0:T(8,128)(2,1)}, f32[1,128,512]{2,1,0:T(8,128)}, f32[16,512]{1,0:T(8,128)}, /*index=5*/f32[16,512]{1,0:T(8,128)}) custom-call(f32[128,512]{1,0:T(8,128)S(1)} %get-tuple-element.10.gradient, f32[1,128,512]{2,1,0:T(8,128)S(1)} %copy-done, ...), custom_call_target="tpu_custom_call" | custom-call | tf_op jit(solution)/shard_map/finish/pallas_call | solution.py:353
Async XLA Ops:
  0.6 54.5 %copy-start.2 = (bf16[1,128,512]{2,1,0:T(8,128)(2,1)S(1)}, bf16[1,128,512]{2,1,0:T(8,128)(2,1)}, u32[]{:S(2)}) copy-start(bf16[1,128,512]{2,1,0:T(8,128)(2,1)} %second.1) | copy-start | bytes 393220
  0.6 54.5 %copy-start.1 = (bf16[1,128,512]{2,1,0:T(8,128)(2,1)S(1)}, bf16[1,128,512]{2,1,0:T(8,128)(2,1)}, u32[]{:S(2)}) copy-start(bf16[1,128,512]{2,1,0:T(8,128)(2,1)} %first.1) | copy-start | bytes 393220
  0.7 54.5 %copy-start = (f32[1,128,512]{2,1,0:T(8,128)S(1)}, f32[1,128,512]{2,1,0:T(8,128)}, u32[]{:S(2)}) copy-start(f32[1,128,512]{2,1,0:T(8,128)} %weight.1) | copy-start | bytes 786436

commit v3 on v2

--- a/solution.py
+++ b/solution.py
@@ -37,23 +37,23 @@
 SLOT = {block: (i, j) for i, pair in enumerate(PAIRS) for j, block in enumerate(pair)}
 
 ORDER = (
-    ("dot", 0), ("y1", 0, 0, 0), ("y1", 0, 0, 1), ("z2", 0, 0, 1), ("z2", 0, 0, 0), ("y1", 1, 0, 1),
-    ("y1", 1, 0, 0), ("dot", 3), ("z2", 3, 0, 1), ("z2", 4, 0, 0), ("z2", 3, 0, 0), ("dot", 1),
-    ("y1", 3, 0, 0), ("z2", 4, 0, 1), ("y1", 2, 0, 1), ("y1", 3, 0, 1), ("y1", 2, 0, 0), ("dot", 2),
-    ("dot", 4), ("z2", 5, 0, 1), ("z2", 1, 0, 0), ("dot", 6), ("z2", 2, 0, 1), ("y1", 0, 1, 0),
-    ("y1", 0, 1, 1), ("dot", 7), ("z2", 2, 0, 0), ("dot", 5), ("z2", 6, 0, 0), ("z2", 1, 0, 1),
-    ("z2", 0, 1, 1), ("y1", 1, 1, 1), ("y1", 1, 1, 0), ("dot", 15), ("z2", 5, 0, 0), ("dot", 10),
-    ("z2", 6, 0, 1), ("y1", 2, 1, 0), ("y1", 2, 1, 1), ("z2", 7, 0, 1), ("z2", 0, 1, 0), ("dot", 14),
-    ("dot", 8), ("z2", 7, 0, 0), ("dot", 9), ("y1", 0, 2, 1), ("z2", 2, 1, 1), ("y1", 0, 2, 0),
-    ("z2", 1, 1, 0), ("z2", 4, 1, 1), ("dot", 12), ("y1", 1, 2, 0), ("z2", 4, 1, 0), ("z2", 3, 1, 1),
-    ("y1", 1, 2, 1), ("y1", 2, 2, 0), ("z2", 2, 1, 0), ("y1", 2, 2, 1), ("z2", 7, 1, 1), ("y1", 0, 3, 1),
-    ("y1", 0, 3, 0), ("dot", 13), ("y2", 0, 1), ("y2", 0, 0), ("z2", 1, 1, 1), ("dot", 11), ("z2", 5, 1, 0),
-    ("z2", 3, 1, 0), ("y1", 1, 3, 0), ("y1", 3, 1, 1), ("y1", 1, 3, 1), ("y1", 3, 1, 0), ("z1", 0, 0),
-    ("y1", 2, 3, 1), ("y1", 2, 3, 0), ("z2", 5, 1, 1), ("z2", 6, 1, 1), ("z2", 7, 1, 0), ("y2", 1, 1),
-    ("y2", 1, 0), ("y1", 3, 2, 1), ("z2", 6, 1, 0), ("y1", 3, 2, 0), ("z1", 1, 0), ("z1", 1, 1),
-    ("y2", 2, 0), ("y2", 2, 1), ("y1", 3, 3, 0), ("y1", 3, 3, 1), ("y2", 3, 0), ("y2", 3, 1), ("z1", 2),
-    ("y2", 4),
+    ("dot", 0), ("y1", 0, 0, 1), ("y1", 0, 0, 0), ("dot", 1), ("z2", 0, 0, 1), ("z2", 0, 0, 0),
+    ("y1", 2, 0, 1), ("y1", 1, 0, 1), ("y1", 2, 0, 0), ("dot", 2), ("z2", 2, 0, 1), ("z2", 2, 0, 0),
+    ("y1", 3, 0, 1), ("y1", 3, 0, 0), ("dot", 5), ("dot", 3), ("z2", 4, 0, 0), ("z2", 1, 0, 1),
+    ("y1", 1, 0, 0), ("z2", 3, 0, 0), ("z2", 7, 0, 1), ("dot", 7), ("y1", 0, 1, 1), ("y1", 0, 1, 0),
+    ("dot", 4), ("z2", 6, 0, 1), ("z2", 6, 0, 0), ("dot", 13), ("dot", 6), ("y1", 2, 1, 0), ("z2", 1, 0, 0),
+    ("y1", 2, 1, 1), ("z2", 4, 0, 1), ("z2", 3, 0, 1), ("y1", 1, 1, 1), ("dot", 12), ("z2", 0, 1, 1),
+    ("z2", 7, 0, 0), ("y1", 1, 1, 0), ("dot", 8), ("dot", 10), ("z2", 5, 0, 0), ("dot", 15), ("dot", 9),
+    ("z2", 0, 1, 0), ("dot", 11), ("y1", 0, 2, 1), ("y1", 0, 2, 0), ("z2", 3, 1, 0), ("z2", 7, 1, 1),
+    ("y1", 2, 2, 1), ("z2", 5, 0, 1), ("z2", 2, 1, 0), ("z2", 4, 1, 0), ("y1", 2, 2, 0), ("z2", 4, 1, 1),
+    ("z2", 2, 1, 1), ("z2", 1, 1, 0), ("y1", 1, 2, 0), ("y1", 1, 2, 1), ("z2", 7, 1, 0), ("y1", 0, 3, 1),
+    ("y1", 0, 3, 0), ("dot", 14), ("z2", 1, 1, 1), ("y1", 2, 3, 1), ("y2", 0, 0), ("y2", 0, 1),
+    ("y1", 3, 1, 1), ("y1", 3, 1, 0), ("z2", 3, 1, 1), ("y1", 1, 3, 1), ("y1", 2, 3, 0), ("z1", 0, 0),
+    ("y1", 1, 3, 0), ("z2", 5, 1, 0), ("y2", 1, 0), ("z2", 5, 1, 1), ("y2", 1, 1), ("y1", 3, 2, 1),
+    ("y1", 3, 2, 0), ("z2", 6, 1, 1), ("z2", 6, 1, 0), ("z1", 1, 0), ("z1", 1, 1), ("y2", 2, 0),
+    ("y2", 2, 1), ("y1", 3, 3, 1), ("y1", 3, 3, 0), ("y2", 3, 0), ("y2", 3, 1), ("z1", 2), ("y2", 4),
 )
+
 
 def kernel(
     hid, cot, chosen, local, anchor, mom,
@@ -95,27 +95,36 @@
         i, j = SLOT[block]
         return ref.at[i, :, j * LANES : (j + 1) * LANES]
 
-    load("cot", cot.at[0], c_own)
-    for block in SLOT:
-        load(block, columns(block, core), half(h_own, block))
-    load("local", local.at[0], l_own)
-    load("anchor", anchor, a_all)
-    load("mom", mom, m_all)
-    pl.semaphore_wait(barrier, len(everyone))
-
     def remote(source, target, send, recv, device):
         return pltpu.make_async_remote_copy(
             src_ref=source, dst_ref=target, send_sem=send, recv_sem=recv,
             device_id=device, device_id_type=pl.DeviceIdType.MESH,
         )
 
-    swaps = {"cot": remote(cot.at[0], c_peer, peer_send.at[0], peer_recv.at[0], peer)}
-    swaps["cot"].start()
-    for i, block in enumerate(SLOT, 1):
-        swaps[block] = remote(
-            columns(block, 1 - core), half(h_peer, block), peer_send.at[i], peer_recv.at[i], peer
-        )
-        swaps[block].start()
+    swaps = {}
+
+    def swap(name, source, target):
+        number = len(swaps)
+        swaps[name] = remote(source, target, peer_send.at[number], peer_recv.at[number], peer)
+        swaps[name].start()
+
+    def swap_blocks(blocks):
+        for block in blocks:
+            swap(block, columns(block, 1 - core), half(h_peer, block))
+
+    def load_blocks(blocks):
+        for block in blocks:
+            load(block, columns(block, core), half(h_own, block))
+
+    blocks = list(SLOT)
+    load("cot", cot.at[0], c_own)
+    pl.semaphore_wait(barrier, len(everyone))
+    swap("cot", cot.at[0], c_peer)
+    swap_blocks(blocks)
+    load_blocks(blocks)
+    load("local", local.at[0], l_own)
+    load("anchor", anchor, a_all)
+    load("mom", mom, m_all)
     spread = []
     for r, device in enumerate(members):
         rows = pl.ds(pl.multiple_of(device[0] * sublength, sublength), sublength)
@@ -123,7 +132,6 @@
             remote(local.at[0, rows], l_in.at[r], group_send.at[r], group_recv.at[r], device)
         )
         spread[-1].start()
-
     loads["cot"].wait()
     ct[0] = jnp.transpose(c_own[...].astype(jnp.float32)).astype(jnp.bfloat16)
     swaps["cot"].wait_recv()

time: 56.3 us -> 54.5 us (0.968)
  the two profiles are of different devices: /device:TPU:66 before, /device:TPU:16 now
where the time goes in v3:
time: 54.5 us; the launch traced here: 54.3 us
  Pallas kernels  52.9 us (97%)
  between operations  1.39 us (3%)
    pallas_call x1, Pallas kernels, reduced(): pl.pallas_call(kernel, out_shape=(jax.ShapeDtypeStruct((rows, keys), f32)...  51.9 us

profile of v3, /device:TPU:16, one launch (start us, length us, event | category | flops | bytes accessed | tf_op | source)
XLA Modules:
  0.0 54.3 jit_solution(2164650898094622795)
XLA Ops:
  0.6 0.0 copy-start.2
  0.6 0.0 copy-start.1
  0.7 0.0 copy-start
  1.4 51.9 %reduce_and_sync.1 = (f32[128,512]{1,0:T(8,128)S(1)}, f32[128,512]{1,0:T(8,128)S(1)}, f32[16,512]{1,0:T(8,128)S(1)}, f32[16,512]{1,0:T(8,128)S(1)}) custom-call(bf16[1,184,8192]{2,1,0:T(8,128)(2,1)} %hid.1, bf16[1,184,512]{2,1,0:T(8,128)(2,1)} %cot.1, s32[1]{0:T(128)S(6)} %copy.15.chosen, f32[1,128,512]{2,1,0:T(8,128)} %local.1, f32[6,16,512]{2,1,0:T(8,128)} %anchor.1, ...), custom_call_target="tpu_custom_call" | custom-call | tf_op jit(solution)/shard_map/reduce_and_sync/pallas_call | solution.py:290
  53.3 0.0 copy-done.2
  53.3 0.0 copy-done.1
  53.3 0.0 copy-done
  53.3 1.0 %finish.1 = (f32[1,128,512]{2,1,0:T(8,128)}, bf16[1,128,512]{2,1,0:T(8,128)(2,1)}, bf16[1,128,512]{2,1,0:T(8,128)(2,1)}, f32[1,128,512]{2,1,0:T(8,128)}, f32[16,512]{1,0:T(8,128)}, /*index=5*/f32[16,512]{1,0:T(8,128)}) custom-call(f32[128,512]{1,0:T(8,128)S(1)} %get-tuple-element.10.gradient, f32[1,128,512]{2,1,0:T(8,128)S(1)} %copy-done, ...), custom_call_target="tpu_custom_call" | custom-call | tf_op jit(solution)/shard_map/finish/pallas_call | solution.py:361
Async XLA Ops:
  0.6 52.6 %copy-start.2 = (bf16[1,128,512]{2,1,0:T(8,128)(2,1)S(1)}, bf16[1,128,512]{2,1,0:T(8,128)(2,1)}, u32[]{:S(2)}) copy-start(bf16[1,128,512]{2,1,0:T(8,128)(2,1)} %second.1) | copy-start | bytes 393220
  0.6 52.6 %copy-start.1 = (bf16[1,128,512]{2,1,0:T(8,128)(2,1)S(1)}, bf16[1,128,512]{2,1,0:T(8,128)(2,1)}, u32[]{:S(2)}) copy-start(bf16[1,128,512]{2,1,0:T(8,128)(2,1)} %first.1) | copy-start | bytes 393220
  0.7 52.6 %copy-start = (f32[1,128,512]{2,1,0:T(8,128)S(1)}, f32[1,128,512]{2,1,0:T(8,128)}, u32[]{:S(2)}) copy-start(f32[1,128,512]{2,1,0:T(8,128)} %weight.1) | copy-start | bytes 786436

commit v4 on v3

--- a/solution.py
+++ b/solution.py
@@ -25,6 +25,8 @@
 H1 = 176
 H2 = 80
 LANES = 128
+Y_FIRST = ((0,), (1,), (2,), (3,))
+Z_FIRST = ((0,), (1, 2), (3, 4), (5, 6, 7))
 
 
 PAIRS = (
@@ -37,21 +39,18 @@
 SLOT = {block: (i, j) for i, pair in enumerate(PAIRS) for j, block in enumerate(pair)}
 
 ORDER = (
-    ("dot", 0), ("y1", 0, 0, 1), ("y1", 0, 0, 0), ("dot", 1), ("z2", 0, 0, 1), ("z2", 0, 0, 0),
-    ("y1", 2, 0, 1), ("y1", 1, 0, 1), ("y1", 2, 0, 0), ("dot", 2), ("z2", 2, 0, 1), ("z2", 2, 0, 0),
-    ("y1", 3, 0, 1), ("y1", 3, 0, 0), ("dot", 5), ("dot", 3), ("z2", 4, 0, 0), ("z2", 1, 0, 1),
-    ("y1", 1, 0, 0), ("z2", 3, 0, 0), ("z2", 7, 0, 1), ("dot", 7), ("y1", 0, 1, 1), ("y1", 0, 1, 0),
-    ("dot", 4), ("z2", 6, 0, 1), ("z2", 6, 0, 0), ("dot", 13), ("dot", 6), ("y1", 2, 1, 0), ("z2", 1, 0, 0),
-    ("y1", 2, 1, 1), ("z2", 4, 0, 1), ("z2", 3, 0, 1), ("y1", 1, 1, 1), ("dot", 12), ("z2", 0, 1, 1),
-    ("z2", 7, 0, 0), ("y1", 1, 1, 0), ("dot", 8), ("dot", 10), ("z2", 5, 0, 0), ("dot", 15), ("dot", 9),
-    ("z2", 0, 1, 0), ("dot", 11), ("y1", 0, 2, 1), ("y1", 0, 2, 0), ("z2", 3, 1, 0), ("z2", 7, 1, 1),
-    ("y1", 2, 2, 1), ("z2", 5, 0, 1), ("z2", 2, 1, 0), ("z2", 4, 1, 0), ("y1", 2, 2, 0), ("z2", 4, 1, 1),
-    ("z2", 2, 1, 1), ("z2", 1, 1, 0), ("y1", 1, 2, 0), ("y1", 1, 2, 1), ("z2", 7, 1, 0), ("y1", 0, 3, 1),
-    ("y1", 0, 3, 0), ("dot", 14), ("z2", 1, 1, 1), ("y1", 2, 3, 1), ("y2", 0, 0), ("y2", 0, 1),
-    ("y1", 3, 1, 1), ("y1", 3, 1, 0), ("z2", 3, 1, 1), ("y1", 1, 3, 1), ("y1", 2, 3, 0), ("z1", 0, 0),
-    ("y1", 1, 3, 0), ("z2", 5, 1, 0), ("y2", 1, 0), ("z2", 5, 1, 1), ("y2", 1, 1), ("y1", 3, 2, 1),
-    ("y1", 3, 2, 0), ("z2", 6, 1, 1), ("z2", 6, 1, 0), ("z1", 1, 0), ("z1", 1, 1), ("y2", 2, 0),
-    ("y2", 2, 1), ("y1", 3, 3, 1), ("y1", 3, 3, 0), ("y2", 3, 0), ("y2", 3, 1), ("z1", 2), ("y2", 4),
+    ("dot", 0), ("y0", 0, 1), ("y0", 0, 0), ("z2", 0, 0, 1), ("dot", 1), ("y0", 1, 0), ("z2", 0, 0, 0),
+    ("y0", 2, 1), ("y0", 2, 0), ("dot", 3), ("z2", 2, 0, 1), ("y0", 3, 1), ("z2", 2, 0, 0), ("dot", 7),
+    ("y0", 3, 0), ("dot", 10), ("dot", 2), ("y0", 1, 1), ("dot", 6), ("dot", 13), ("y1", 0, 1, 1),
+    ("y1", 0, 1, 0), ("dot", 4), ("z2", 1, 0, 1), ("z2", 1, 0, 0), ("dot", 8), ("y1", 2, 1, 1), ("dot", 5),
+    ("dot", 9), ("y1", 1, 1, 0), ("z2", 0, 1, 1), ("z2", 0, 1, 0), ("y1", 1, 1, 1), ("dot", 12),
+    ("y1", 2, 1, 0), ("z2", 3, 0, 0), ("z2", 3, 0, 1), ("y1", 0, 2, 1), ("y1", 0, 2, 0), ("y1", 1, 2, 0),
+    ("z2", 2, 1, 1), ("z2", 1, 1, 0), ("y1", 2, 2, 1), ("y2", 0, 0), ("y2", 0, 1), ("z2", 1, 1, 1),
+    ("y1", 0, 3, 1), ("y1", 0, 3, 0), ("dot", 15), ("y1", 1, 2, 1), ("y1", 2, 2, 0), ("dot", 14),
+    ("z2", 2, 1, 0), ("dot", 11), ("y1", 3, 1, 0), ("y1", 2, 3, 1), ("y1", 1, 3, 0), ("y1", 3, 1, 1),
+    ("z1", 0, 0), ("y1", 1, 3, 1), ("z2", 3, 1, 0), ("z2", 3, 1, 1), ("y1", 2, 3, 0), ("y2", 1, 0),
+    ("y2", 1, 1), ("y1", 3, 2, 0), ("y1", 3, 2, 1), ("z1", 1, 0), ("z1", 1, 1), ("y2", 2, 0), ("y2", 2, 1),
+    ("y1", 3, 3, 1), ("y1", 3, 3, 0), ("y2", 3, 0), ("y2", 3, 1), ("y2", 4), ("z1", 2),
 )
 
 
@@ -137,20 +136,32 @@
     swaps["cot"].wait_recv()
     ct[1] = jnp.transpose(c_peer[...].astype(jnp.float32)).astype(jnp.bfloat16)
 
-    messages = {}
+    copies, messages, landed = [], {}, set()
+
+    def depart(axis, d, out, into):
+        number = len(copies)
+        copies.append(remote(out, into, send_sem.at[number], recv_sem.at[number], partner[axis][d]))
+        copies[-1].start()
+        return number
 
     def send(name, axis, d, bufs, index, value):
-        number = len(messages)
         out, into = bufs.at[(0,) + index], bufs.at[(1,) + index]
         out[...] = value.astype(jnp.bfloat16)
-        messages[name] = (
-            remote(out, into, send_sem.at[number], recv_sem.at[number], partner[axis][d]), into,
-        )
-        messages[name][0].start()
+        messages[name] = (depart(axis, d, out, into), into)
+
+    def send_strips(names, axis, d, bufs, index, strips, values):
+        for strip, value in zip(strips, values):
+            bufs[(0,) + index + (strip,)] = value.astype(jnp.bfloat16)
+        side = (pl.ds(strips[0], len(strips)),)
+        number = depart(axis, d, bufs.at[(0,) + index + side], bufs.at[(1,) + index + side])
+        for name, strip in zip(names, strips):
+            messages[name] = (number, bufs.at[(1,) + index + (strip,)])
 
     def arrived(name):
-        copy, into = messages[name]
-        copy.wait_recv()
+        number, into = messages[name]
+        if number not in landed:
+            landed.add(number)
+            copies[number].wait_recv()
         return into[...].astype(jnp.float32)
 
     def own(dy, dz, begin, end):
@@ -171,12 +182,16 @@
             ct[1], h_peer[i], preferred_element_type=jnp.float32
         )
 
+    def step_y0(group, d):
+        begin, end = ((0, H1), (H1, R1))[d]
+        strips = Y_FIRST[group]
+        send_strips(
+            [("y1", s, 0, d) for s in strips], "y", d, (y1a, y1b)[d], (), strips,
+            [own(4, DZS[s], begin, end) for s in strips],
+        )
+
     def step_y1(s, h, d):
         dz = DZS[s]
-        if h == 0:
-            begin, end = ((0, H1), (H1, R1))[d]
-            send(("y1", s, h, d), "y", d, (y1a, y1b)[d], (s,), own(4, dz, begin, end))
-            return
         whole = own(SIGN[d] * (4 - h), dz, 0, R1)
         if h == 1:
             whole = with_part(("y1", s, 0, d), d, whole, H1)
@@ -198,14 +213,16 @@
         else:
             fin[0:R1, :] = y1_sum(3) + arrived(("z1", 1, UP)) + arrived(("z1", 1, DOWN))
 
-    def step_z2(k, h, d):
-        dy = DYS[k]
+    def step_z2(group, h, d):
+        strips = Z_FIRST[group]
+        names = [("z2", k, h, d) for k in strips]
         if h == 0:
             begin, end = ((R1, R1 + H2), (R1 + H2, 512))[d]
-            send(("z2", k, h, d), "z", d, (z2a, z2b)[d], (k,), own(dy, 2, begin, end))
+            values = [own(DYS[k], 2, begin, end) for k in strips]
+            send_strips(names, "z", d, (z2a, z2b)[d], (), strips, values)
             return
-        whole = with_part(("z2", k, 0, d), d, own(dy, SIGN[d], R1, 512), H2)
-        send(("z2", k, h, d), "z", d, z2w, (d, k), whole)
+        values = [with_part(("z2", k, 0, d), d, own(DYS[k], SIGN[d], R1, 512), H2) for k in strips]
+        send_strips(names, "z", d, z2w, (d,), strips, values)
 
     def z2_sum(k):
         return own(DYS[k], 0, R1, 512) + arrived(("z2", k, 1, UP)) + arrived(("z2", k, 1, DOWN))
@@ -261,7 +278,7 @@
             rows = pl.ds(pl.multiple_of(source * sublength, sublength), sublength)
             local_out[rows, :] = mixing * l_own[rows, :] + (1.0 - mixing) * a_in[r].astype(jnp.float32)
 
-    run = {"dot": step_dot, "y1": step_y1, "z1": step_z1, "z2": step_z2, "y2": step_y2}
+    run = {"dot": step_dot, "y0": step_y0, "y1": step_y1, "z1": step_z1, "z2": step_z2, "y2": step_y2}
     for number, name in enumerate(ORDER):
         if number == len(ORDER) // 2:
             outer_first()
@@ -270,7 +287,7 @@
         run[name[0]](*name[1:])
 
     grad_out[...] = jnp.transpose(fin[...])
-    for copy in list(swaps.values()) + spread + returned + [copy for copy, _ in messages.values()]:
+    for copy in list(swaps.values()) + spread + returned + copies:
         copy.wait_send()
 
 

time: 54.5 us -> 54.1 us (level)
  the two profiles are of different devices: /device:TPU:16 before, /device:TPU:2 now
where the time goes in v4:
time: 54.1 us; the launch traced here: 54 us
  Pallas kernels  52.5 us (97%)
  between operations  1.39 us (3%)
    pallas_call x1, Pallas kernels, reduced(): pl.pallas_call(kernel, out_shape=(jax.ShapeDtypeStruct((rows, keys), f32)...  51.5 us

profile of v4, /device:TPU:2, one launch (start us, length us, event | category | flops | bytes accessed | tf_op | source)
XLA Modules:
  0.0 54.0 jit_solution(1194980182206789088)
XLA Ops:
  0.6 0.0 copy-start.2
  0.6 0.0 copy-start.1
  0.7 0.0 copy-start
  1.4 51.5 %reduce_and_sync.1 = (f32[128,512]{1,0:T(8,128)S(1)}, f32[128,512]{1,0:T(8,128)S(1)}, f32[16,512]{1,0:T(8,128)S(1)}, f32[16,512]{1,0:T(8,128)S(1)}) custom-call(bf16[1,184,8192]{2,1,0:T(8,128)(2,1)} %hid.1, bf16[1,184,512]{2,1,0:T(8,128)(2,1)} %cot.1, s32[1]{0:T(128)S(6)} %copy.15.chosen, f32[1,128,512]{2,1,0:T(8,128)} %local.1, f32[6,16,512]{2,1,0:T(8,128)} %anchor.1, ...), custom_call_target="tpu_custom_call" | custom-call | tf_op jit(solution)/shard_map/reduce_and_sync/pallas_call | solution.py:307
  52.9 0.0 copy-done.2
  52.9 0.0 copy-done.1
  52.9 0.0 copy-done
  52.9 1.0 %finish.1 = (f32[1,128,512]{2,1,0:T(8,128)}, bf16[1,128,512]{2,1,0:T(8,128)(2,1)}, bf16[1,128,512]{2,1,0:T(8,128)(2,1)}, f32[1,128,512]{2,1,0:T(8,128)}, f32[16,512]{1,0:T(8,128)}, /*index=5*/f32[16,512]{1,0:T(8,128)}) custom-call(f32[128,512]{1,0:T(8,128)S(1)} %get-tuple-element.10.gradient, f32[1,128,512]{2,1,0:T(8,128)S(1)} %copy-done, ...), custom_call_target="tpu_custom_call" | custom-call | tf_op jit(solution)/shard_map/finish/pallas_call | solution.py:378
Async XLA Ops:
  0.6 52.2 %copy-start.2 = (bf16[1,128,512]{2,1,0:T(8,128)(2,1)S(1)}, bf16[1,128,512]{2,1,0:T(8,128)(2,1)}, u32[]{:S(2)}) copy-start(bf16[1,128,512]{2,1,0:T(8,128)(2,1)} %second.1) | copy-start | bytes 393220
  0.6 52.2 %copy-start.1 = (bf16[1,128,512]{2,1,0:T(8,128)(2,1)S(1)}, bf16[1,128,512]{2,1,0:T(8,128)(2,1)}, u32[]{:S(2)}) copy-start(bf16[1,128,512]{2,1,0:T(8,128)(2,1)} %first.1) | copy-start | bytes 393220
  0.7 52.2 %copy-start = (f32[1,128,512]{2,1,0:T(8,128)S(1)}, f32[1,128,512]{2,1,0:T(8,128)}, u32[]{:S(2)}) copy-start(f32[1,128,512]{2,1,0:T(8,128)} %weight.1) | copy-start | bytes 786436

commit v5 on v4

--- a/solution.py
+++ b/solution.py
@@ -208,10 +208,20 @@
             send(("z1", 0, UP), "z", UP, z1a, (), whole[:H1])
             send(("z1", 0, DOWN), "z", DOWN, z1b, (), whole[H1:])
         elif h == 1:
-            whole = with_part(("z1", 0, d), d, y1_sum(1 + d), H1)
-            send(("z1", 1, d), "z", d, z1w, (d,), whole)
+            whole = y1_sum(1 + d)
+            rows = ((0, H1), (H1, R1))
+            for side in (1 - d, d):
+                begin, end = rows[side]
+                value = whole[begin:end]
+                if side == d:
+                    value = value + arrived(("z1", 0, d))
+                place_of = (d, pl.ds(begin, end - begin))
+                send(("z1", 1, d, side), "z", d, z1w, place_of, value)
         else:
-            fin[0:R1, :] = y1_sum(3) + arrived(("z1", 1, UP)) + arrived(("z1", 1, DOWN))
+            for side, (begin, end) in enumerate(((0, H1), (H1, R1))):
+                fin[begin:end, :] = (
+                    y1_sum(3)[begin:end] + arrived(("z1", 1, UP, side)) + arrived(("z1", 1, DOWN, side))
+                )
 
     def step_z2(group, h, d):
         strips = Z_FIRST[group]

time: 54.1 us -> 54.1 us (level)
  no operation moved by 1% of the time
where the time goes in v5:
time: 54.1 us; the launch traced here: 53.9 us
  Pallas kernels  52.5 us (97%)
  between operations  1.39 us (3%)
    pallas_call x1, Pallas kernels, reduced(): pl.pallas_call(kernel, out_shape=(jax.ShapeDtypeStruct((rows, keys), f32)...  51.5 us

profile of v5, /device:TPU:2, one launch (start us, length us, event | category | flops | bytes accessed | tf_op | source)
XLA Modules:
  0.0 53.9 jit_solution(8978462027023658343)
XLA Ops:
  0.6 0.0 copy-start.2
  0.6 0.0 copy-start.1
  0.7 0.0 copy-start
  1.4 51.5 %reduce_and_sync.1 = (f32[128,512]{1,0:T(8,128)S(1)}, f32[128,512]{1,0:T(8,128)S(1)}, f32[16,512]{1,0:T(8,128)S(1)}, f32[16,512]{1,0:T(8,128)S(1)}) custom-call(bf16[1,184,8192]{2,1,0:T(8,128)(2,1)} %hid.1, bf16[1,184,512]{2,1,0:T(8,128)(2,1)} %cot.1, s32[1]{0:T(128)S(6)} %copy.15.chosen, f32[1,128,512]{2,1,0:T(8,128)} %local.1, f32[6,16,512]{2,1,0:T(8,128)} %anchor.1, ...), custom_call_target="tpu_custom_call" | custom-call | tf_op jit(solution)/shard_map/reduce_and_sync/pallas_call | solution.py:317
  52.9 0.0 copy-done.2
  52.9 0.0 copy-done.1
  52.9 0.0 copy-done
  52.9 1.0 %finish.1 = (f32[1,128,512]{2,1,0:T(8,128)}, bf16[1,128,512]{2,1,0:T(8,128)(2,1)}, bf16[1,128,512]{2,1,0:T(8,128)(2,1)}, f32[1,128,512]{2,1,0:T(8,128)}, f32[16,512]{1,0:T(8,128)}, /*index=5*/f32[16,512]{1,0:T(8,128)}) custom-call(f32[128,512]{1,0:T(8,128)S(1)} %get-tuple-element.10.gradient, f32[1,128,512]{2,1,0:T(8,128)S(1)} %copy-done, ...), custom_call_target="tpu_custom_call" | custom-call | tf_op jit(solution)/shard_map/finish/pallas_call | solution.py:388
Async XLA Ops:
  0.6 52.2 %copy-start.2 = (bf16[1,128,512]{2,1,0:T(8,128)(2,1)S(1)}, bf16[1,128,512]{2,1,0:T(8,128)(2,1)}, u32[]{:S(2)}) copy-start(bf16[1,128,512]{2,1,0:T(8,128)(2,1)} %second.1) | copy-start | bytes 393220
  0.6 52.2 %copy-start.1 = (bf16[1,128,512]{2,1,0:T(8,128)(2,1)S(1)}, bf16[1,128,512]{2,1,0:T(8,128)(2,1)}, u32[]{:S(2)}) copy-start(bf16[1,128,512]{2,1,0:T(8,128)(2,1)} %first.1) | copy-start | bytes 393220
  0.7 52.2 %copy-start = (f32[1,128,512]{2,1,0:T(8,128)S(1)}, f32[1,128,512]{2,1,0:T(8,128)}, u32[]{:S(2)}) copy-start(f32[1,128,512]{2,1,0:T(8,128)} %weight.1) | copy-start | bytes 786436
